TPU v7x, 128 devices: a whole 4x4x4 slice. The times are simulated.
128 devices in a mesh: ia: 2 (over z_hi), ja: 8 (over x, core), ka: 8 (over y, z_lo).
Axes of the slice: x: 4, y: 4, z: 4 (z_hi: 2, z_lo: 2; z = z_hi * 2 + z_lo), core: 2. Of those that a mesh axis runs over, the one named last changes fastest.
Arguments:
- hidden_act: bfloat16 [768, 26624], P(('ia', 'ka'), 'ja'), may hold values from -6 to 6
- w_down: bfloat16 [26624, 16384], P('ja', ('ia', 'ka')), may hold values from -0.0390625 to 0.0390625
- w_out: bfloat16 [16384, 16384], P(('ia', 'ka'), 'ja'), may hold values from -0.046875 to 0.046875
- head_grad: bfloat16 [768, 16384], P(('ia', 'ka'), 'ja'), may hold values from -6 to 6
- token_ratio: float32 [768], P(('ia', 'ka')), may hold values from -4 to 4
- pair_slot: int32 [768], P(('ia', 'ka')), may hold values from 0 to 15
- segment_id: int32 [768], P(('ia', 'ka')), may hold values from 0 to 191, never falling along the last dimension, each value on 1 to 16 neighbouring positions
Outputs:
- projected: bfloat16 [768, 16384], P(('ia', 'ka'), 'ja')
- grad_hidden: bfloat16 [768, 26624], P(('ia', 'ka'), 'ja')
- grad_down: bfloat16 [26624, 16384], P('ja', ('ia', 'ka'))
- grad_out: bfloat16 [16384, 16384], P(('ia', 'ka'), 'ja')
All inputs are finite; a program needn't handle non-finite values.
Results may differ from a plain program's by a relative error of at most 0.0058.
Values may be sent and summed in bfloat16 or wider, within the bound.
A program may use at most 128 MiB of HBM per device.

v0:
```python
import jax
import jax.numpy as jnp
from jax import lax
from jax.sharding import PartitionSpec as P

PAIRS = 8
beta_scale = 0.5


def gather_rows(block):
    return lax.all_gather(block, ("ia", "ka"), axis=0, tiled=True)


def scatter_rows(term, local_rows):
    return lax.psum_scatter(
        term(jnp.int32(0), local_rows * lax.axis_size(("ia", "ka"))),
        ("ia", "ka"),
        scatter_dimension=0,
        tiled=True,
    )


def summed_middle(term, total_rows):
    shares = lax.psum_scatter(
        term(jnp.int32(0), total_rows // lax.axis_size("ja") * lax.axis_size("ja")),
        "ja",
        scatter_dimension=0,
        tiled=True,
    ).astype(jnp.bfloat16)
    return lax.all_gather(shares, "ja", axis=0, tiled=True)


def contract_last(left, right):
    return lax.dot_general(
        left, right, (((1,), (1,)), ((), ())), preferred_element_type=jnp.float32
    )


def contract_first(left, right):
    return lax.dot_general(
        left, right, (((0,), (0,)), ((), ())), preferred_element_type=jnp.float32
    )


def local(hidden_act, w_down, w_out, head_grad, token_ratio, pair_slot, segment_id):
    local_rows = hidden_act.shape[0]
    total_rows = local_rows * lax.axis_size("ia") * lax.axis_size("ka")
    full_hidden = gather_rows(hidden_act)

    def down_term(start, count):
        return jnp.dot(full_hidden, w_down, preferred_element_type=jnp.float32)

    down_full = summed_middle(down_term, total_rows)

    def out_term(start, count):
        return jnp.dot(down_full, w_out, preferred_element_type=jnp.float32)

    projected = scatter_rows(out_term, local_rows).astype(jnp.bfloat16)
    masked = (segment_id % 2).astype(jnp.float32)
    signed = masked * (1 - 2 * (pair_slot % 2)).astype(jnp.float32)
    onehot = ((pair_slot // 2)[:, None] == jnp.arange(PAIRS, dtype=jnp.int32)[None, :]).astype(
        jnp.float32
    )
    local_margin = jnp.dot(signed * token_ratio, onehot, precision=lax.Precision.HIGHEST)
    margin = lax.psum(local_margin, ("ia", "ka"))
    pair_weight = -beta_scale * jax.nn.sigmoid(-beta_scale * margin)
    coef = jnp.dot(onehot, pair_weight, precision=lax.Precision.HIGHEST) * signed
    cotangent = (coef[:, None] * head_grad.astype(jnp.float32)).astype(jnp.bfloat16)
    full_cotangent = gather_rows(cotangent)

    def back_term(start, count):
        return contract_last(full_cotangent, w_out)

    grad_mid = summed_middle(back_term, total_rows)
    grad_out = contract_first(down_full, full_cotangent).astype(jnp.bfloat16)

    def hidden_term(start, count):
        return contract_last(grad_mid, w_down)

    grad_hidden = scatter_rows(hidden_term, local_rows).astype(jnp.bfloat16)
    grad_down = contract_first(full_hidden, grad_mid).astype(jnp.bfloat16)
    return (projected, grad_hidden, grad_down, grad_out)


def solution(mesh):
    placed = (
        P(("ia", "ka"), "ja"),
        P("ja", ("ia", "ka")),
        P(("ia", "ka"), "ja"),
        P(("ia", "ka"), "ja"),
        P(("ia", "ka")),
        P(("ia", "ka")),
        P(("ia", "ka")),
    )
    return jax.shard_map(
        local,
        mesh=mesh,
        in_specs=placed,
        out_specs=(
            P(("ia", "ka"), "ja"),
            P(("ia", "ka"), "ja"),
            P("ja", ("ia", "ka")),
            P(("ia", "ka"), "ja"),
        ),
        check_vma=False,
    )
```

profile of v0, /device:TPU:9, one launch (start us, length us, event | category | flops | bytes accessed | tf_op | source)
XLA Modules:
  0.0 708.8 jit_solution(12141324303579329130)
XLA Ops:
  7.2 0.0 all-gather.5.cloned.1.call-start
  7.2 0.7 all-gather.5.cloned.1.call-update
  7.9 0.0 all-gather.9.cloned.1.call-start
  7.9 0.7 and_select_fusion.2
  8.6 0.7 fusion.5
  9.3 0.8 convolution_bitcast_fusion.1
  10.1 33.9 %psum.7 = f32[8]{0:T(128)S(1)} all-reduce(f32[8]{0:T(128)S(1)} %convolution_bitcast_fusion.1), channel_id=1, replica_groups=mesh['ia'=2,'ja'=8,'ka'=8] {'ia','ka'}, use_global_device_ids=true, to_apply=%region_2.3 | all-reduce | flops 8 | bytes 64 | tf_op jit(solution)/shard_map/psum | solution.py:65
  44.0 0.2 fusion.1
  44.2 1.7 multiply_convert_fusion
  45.9 0.0 all-gather.9.cloned.1.call-update
  46.0 0.0 reduce-scatter.5.cloned.1.call-start
  46.0 81.2 %all-gather.5.cloned.1.call-done = bf16[768,3328]{1,0:T(8,128)(2,1)} async-done(((bf16[48,3328]{1,0:T(8,128)(2,1)}), bf16[768,3328]{1,0:T(8,128)(2,1)}) %all-gather.5.cloned.1.call-update) | async-done | bytes 5111824 | tf_op jit(solution)/shard_map/all_gather | solution.py:11
  127.2 10.2 %fusion.19 = f32[768,1024]{1,0:T(8,128)} fusion(bf16[768,3328]{1,0:T(8,128)(2,1)} %all-gather.5.cloned.1.call-done, bf16[3328,1024]{1,0:T(8,128)(2,1)} %param.8), kind=kOutput, calls=%fused_computation.35 | convolution fusion | flops 5234491392 | bytes 15073280 | tf_op jit(solution)/shard_map/dot_general | solution.py:51
  137.4 0.0 reduce-scatter.5.cloned.1.call-update
  137.5 0.0 reduce-scatter.9.cloned.1.call-start
  137.5 68.5 %all-gather.9.cloned.1.call-done = bf16[768,2048]{1,0:T(8,128)(2,1)} async-done(((bf16[48,2048]{1,0:T(8,128)(2,1)}), bf16[768,2048]{1,0:T(8,128)(2,1)}) %all-gather.9.cloned.1.call-update) | async-done | bytes 3145744 | tf_op jit(solution)/shard_map/all_gather | solution.py:11
  206.0 8.3 %fusion.21 = f32[768,1024]{1,0:T(8,128)} fusion(bf16[768,2048]{1,0:T(8,128)(2,1)} %all-gather.9.cloned.1.call-done, bf16[1024,2048]{1,0:T(8,128)(2,1)} %param.9), kind=kOutput, calls=%fused_computation.37 | convolution fusion | flops 3221225472 | bytes 10485760 | tf_op jit(solution)/shard_map/dot_general | solution.py:34
  214.2 0.0 reduce-scatter.9.cloned.1.call-update
  214.3 0.0 all-gather.7.cloned.1.call-start
  214.3 31.8 %reduce-scatter.5.cloned.1.call-done = f32[96,1024]{1,0:T(8,128)} async-done(((f32[768,1024]{1,0:T(8,128)}), f32[96,1024]{1,0:T(8,128)}) %reduce-scatter.5.cloned.1.call-update) | async-done | bytes 393232 | tf_op jit(solution)/shard_map/reduce_scatter | solution.py:24
  246.1 1.7 convert_element_type.34
  247.8 0.0 all-gather.7.cloned.1.call-update
  247.8 0.0 all-gather.11.cloned.1.call-start
  247.9 35.6 %reduce-scatter.9.cloned.1.call-done = f32[96,1024]{1,0:T(8,128)} async-done(((f32[768,1024]{1,0:T(8,128)}), f32[96,1024]{1,0:T(8,128)}) %reduce-scatter.9.cloned.1.call-update) | async-done | bytes 393232 | tf_op jit(solution)/shard_map/reduce_scatter | solution.py:24
  283.5 1.7 convert_element_type.40
  285.2 0.0 all-gather.11.cloned.1.call-update
  285.2 0.0 reduce-scatter.7.cloned.1.call-start
  285.3 27.0 %all-gather.7.cloned.1.call-done = bf16[768,1024]{1,0:T(8,128)(2,1)} async-done(((bf16[96,1024]{1,0:T(8,128)(2,1)}), bf16[768,1024]{1,0:T(8,128)(2,1)}) %all-gather.7.cloned.1.call-update) | async-done | bytes 1572880 | tf_op jit(solution)/shard_map/all_gather | solution.py:30
  312.3 8.7 %fusion.20 = f32[768,2048]{1,0:T(8,128)} fusion(bf16[768,1024]{1,0:T(8,128)(2,1)} %all-gather.7.cloned.1.call-done, bf16[1024,2048]{1,0:T(8,128)(2,1)} %param.9), kind=kOutput, calls=%fused_computation.36 | convolution fusion | flops 3221225472 | bytes 12058624 | tf_op jit(solution)/shard_map/dot_general | solution.py:56
  321.0 0.0 reduce-scatter.7.cloned.1.call-update
  321.0 0.2 reduce-scatter.11.cloned.1.call-start
  321.2 17.9 %all-gather.11.cloned.1.call-done = bf16[768,1024]{1,0:T(8,128)(2,1)} async-done(((bf16[96,1024]{1,0:T(8,128)(2,1)}), bf16[768,1024]{1,0:T(8,128)(2,1)}) %all-gather.11.cloned.1.call-update) | async-done | bytes 1572880 | tf_op jit(solution)/shard_map/all_gather | solution.py:30
  339.1 11.2 %fusion.22 = f32[768,3328]{1,0:T(8,128)} fusion(bf16[768,1024]{1,0:T(8,128)(2,1)} %all-gather.11.cloned.1.call-done, bf16[3328,1024]{1,0:T(8,128)(2,1)} %param.8), kind=kOutput, calls=%fused_computation.38 | convolution fusion | flops 5234491392 | bytes 18612224 | tf_op jit(solution)/shard_map/dot_general | solution.py:34
  350.3 0.0 copy-start.1
  350.3 0.0 reduce-scatter.11.cloned.1.call-update
  350.3 1.4 copy-done.1
  351.7 9.9 %fusion = bf16[3328,1024]{0,1:T(8,128)(2,1)} fusion(bf16[768,1024]{1,0:T(8,128)(2,1)S(1)} %copy-done.1, bf16[768,3328]{1,0:T(8,128)(2,1)} %all-gather.5.cloned.1.call-done), kind=kOutput, calls=%fused_computation.1 | convolution fusion | flops 5237899264 | bytes 13500416 | tf_op jit(solution)/shard_map/dot_general | solution.py:40
  361.6 0.0 copy-start
  361.6 10.1 %copy.11 = bf16[3328,1024]{1,0:T(8,128)(2,1)} copy(bf16[3328,1024]{0,1:T(8,128)(2,1)} %fusion) | data formatting | bytes 13631488
  371.7 0.0 copy-done
  371.7 6.4 convolution_convert_fusion.1
  378.2 101.3 %reduce-scatter.7.cloned.1.call-done = f32[48,2048]{1,0:T(8,128)} async-done(((f32[768,2048]{1,0:T(8,128)}), f32[48,2048]{1,0:T(8,128)}) %reduce-scatter.7.cloned.1.call-update) | async-done | bytes 393232 | tf_op jit(solution)/shard_map/reduce_scatter | solution.py:15
  479.5 1.7 convert_element_type.35
  481.2 218.9 %reduce-scatter.11.cloned.1.call-done = f32[48,3328]{1,0:T(8,128)} async-done(((f32[768,3328]{1,0:T(8,128)}), f32[48,3328]{1,0:T(8,128)}) %reduce-scatter.11.cloned.1.call-update) | async-done | bytes 638992 | tf_op jit(solution)/shard_map/reduce_scatter | solution.py:15
  700.1 1.8 convert_element_type.41
Async XLA Ops:
  7.2 120.0 %all-gather.5.cloned.1.call-start = ((), (), s32[]{:S(2)}) async-start(), calls=%async_computation.4 | async-start | bytes 5431296 | tf_op jit(solution)/shard_map/all_gather | solution.py:11
  7.9 198.1 %all-gather.9.cloned.1.call-start = ((), (), s32[]{:S(2)}) async-start(), calls=%async_computation.8 | async-start | bytes 3342336 | tf_op jit(solution)/shard_map/all_gather | solution.py:11
  46.0 200.1 %reduce-scatter.5.cloned.1.call-start = ((), (), s32[]{:S(2)}) async-start(), calls=%async_computation.5 | async-start | bytes 3538944 | tf_op jit(solution)/shard_map/reduce_scatter | solution.py:24
  137.5 146.0 %reduce-scatter.9.cloned.1.call-start = ((), (), s32[]{:S(2)}) async-start(), calls=%async_computation.9 | async-start | bytes 3538944 | tf_op jit(solution)/shard_map/reduce_scatter | solution.py:24
  214.3 98.0 %all-gather.7.cloned.1.call-start = ((), (), s32[]{:S(2)}) async-start(), calls=%async_computation.6 | async-start | bytes 1769472 | tf_op jit(solution)/shard_map/all_gather | solution.py:30
  247.8 91.3 %all-gather.11.cloned.1.call-start = ((), (), s32[]{:S(2)}) async-start(), calls=%async_computation.10 | async-start | bytes 1769472 | tf_op jit(solution)/shard_map/all_gather | solution.py:30
  285.2 194.3 %reduce-scatter.7.cloned.1.call-start = ((), (), s32[]{:S(2)}) async-start(), calls=%async_computation.7 | async-start | bytes 6684672 | tf_op jit(solution)/shard_map/reduce_scatter | solution.py:15
  321.0 379.1 %reduce-scatter.11.cloned.1.call-start = ((), (), s32[]{:S(2)}) async-start(), calls=%async_computation.11 | async-start | bytes 10862592 | tf_op jit(solution)/shard_map/reduce_scatter | solution.py:15
  350.3 1.4 copy-start.1
  361.6 10.1 %copy-start = (bf16[768,2048]{1,0:T(8,128)(2,1)S(1)}, bf16[768,2048]{1,0:T(8,128)(2,1)}, u32[]{:S(2)}) copy-start(bf16[768,2048]{1,0:T(8,128)(2,1)} %all-gather.9.cloned.1.call-done) | copy-start | bytes 9437188
Sparse Core Ops, SparseCore 0:
  9.6 117.5 all-gather.4
  129.4 76.5 all-gather.8
  209.0 37.0 reduce-scatter.4
  248.9 34.5 reduce-scatter.8
  285.6 26.6 all-gather.6
  314.4 24.6 all-gather.10
  341.5 137.9 reduce-scatter.6
  481.9 218.1 reduce-scatter.10
where the time goes:
time: 709 us
  waiting for transfers between devices  583 us (82%)
  matrix products  55.8 us (8%)
  blocking collectives  33.9 us (5%)
  between operations  14.1 us (2%)
  local copies, waits for them, and re-layouts  11.5 us (2%)
  other arithmetic  10 us (1%)
    reduce_scatter x2, waiting for transfers between devices, scatter_rows(): lax.psum_scatter(term(jnp.int32(0), local_rows * lax.axis_size(('ia', 'ka...  320 us
    all_gather x2, waiting for transfers between devices, gather_rows(): return lax.all_gather(block, ('ia', 'ka'), axis=0, tiled=True)  150 us
    reduce_scatter x2, waiting for transfers between devices, summed_middle(): lax.psum_scatter(term(jnp.int32(0), total_rows // lax.axis_size('ja') * l...  67.4 us
    all_gather x2, waiting for transfers between devices, summed_middle(): return lax.all_gather(shares, 'ja', axis=0, tiled=True)  44.8 us
    psum x1, blocking collectives, local(): margin = lax.psum(local_margin, ('ia', 'ka'))  33.9 us
    dot_general x2, matrix products, contract_last(): lax.dot_general(left, right, (((1,), (1,)), ((), ())), preferred_element_...  19.4 us
    dot_general x2, matrix products, contract_first(): lax.dot_general(left, right, (((0,), (0,)), ((), ())), preferred_element_...  16.3 us
  transfers between devices with their start and end apart: 8, of which 8 were waited for; matrix products, arithmetic and copies ran while one was open for 10% of the time, Pallas kernels for 0%

commit v1 on v0

--- a/solution.py
+++ b/solution.py
@@ -5,6 +5,12 @@
 
 PAIRS = 8
 beta_scale = 0.5
+
+
+def tiled_gather(x, axis, dim):
+    size = lax.axis_size(axis)
+    repeats = [size if d == dim else 1 for d in range(x.ndim)]
+    return lax.all_to_all(jnp.tile(x, repeats), axis, split_axis=dim, concat_axis=dim, tiled=True)
 
 
 def gather_rows(block):
@@ -27,7 +33,7 @@
         scatter_dimension=0,
         tiled=True,
     ).astype(jnp.bfloat16)
-    return lax.all_gather(shares, "ja", axis=0, tiled=True)
+    return tiled_gather(shares, "ja", 0)
 
 
 def contract_last(left, right):

time: 709 us -> 666 us (0.939)
  waiting for transfers between devices: 583 us -> 487 us
  blocking collectives: 33.9 us -> 92.2 us
    all_to_all x0 -> x2, blocking collectives: none -> 58.4 us  [tiled_gather(): lax.all_to_all(jnp.tile(x, repeats), axis, split_axis=dim, concat_axis=di...]
    all_gather x2 -> x0, waiting for transfers between devices: 44.8 us -> none  [summed_middle(): return lax.all_gather(shares, 'ja', axis=0, tiled=True)]
    reduce_scatter x2, waiting for transfers between devices: 67.4 us -> 40.2 us  [summed_middle(): lax.psum_scatter(term(jnp.int32(0), total_rows // lax.axis_size('ja') * l...]
    reduce_scatter x2, waiting for transfers between devices: 320 us -> 296 us  [scatter_rows(): lax.psum_scatter(term(jnp.int32(0), local_rows * lax.axis_size(('ia', 'ka...]
  transfers between devices with their start and end apart: 8 -> 6, of which waited for: 8 -> 6; matrix products, arithmetic and copies ran while one was open for 10% -> 11% of each run, Pallas kernels for 0% -> 0%
where the time goes in v1:
time: 666 us; the launch traced here: 665 us
  waiting for transfers between devices  487 us (73%)
  blocking collectives  92.2 us (14%)
  matrix products  52.8 us (8%)
  between operations  14.1 us (2%)
  local copies, waits for them, and re-layouts  10.3 us (2%)
  other arithmetic  8.8 us (1%)
    reduce_scatter x2, waiting for transfers between devices, scatter_rows(): lax.psum_scatter(term(jnp.int32(0), local_rows * lax.axis_size(('ia', 'ka...  296 us
    all_gather x2, waiting for transfers between devices, gather_rows(): return lax.all_gather(block, ('ia', 'ka'), axis=0, tiled=True)  150 us
    all_to_all x2, blocking collectives, tiled_gather(): lax.all_to_all(jnp.tile(x, repeats), axis, split_axis=dim, concat_axis=di...  58.4 us
    reduce_scatter x2, waiting for transfers between devices, summed_middle(): lax.psum_scatter(term(jnp.int32(0), total_rows // lax.axis_size('ja') * l...  40.2 us
    psum x1, blocking collectives, local(): margin = lax.psum(local_margin, ('ia', 'ka'))  33.9 us
    dot_general x2, matrix products, contract_last(): lax.dot_general(left, right, (((1,), (1,)), ((), ())), preferred_element_...  19.3 us
    dot_general x2, matrix products, contract_first(): lax.dot_general(left, right, (((0,), (0,)), ((), ())), preferred_element_...  16.9 us
  transfers between devices with their start and end apart: 6, of which 6 were waited for; matrix products, arithmetic and copies ran while one was open for 11% of the time, Pallas kernels for 0%

profile of v1, /device:TPU:9, one launch (start us, length us, event | category | flops | bytes accessed | tf_op | source)
XLA Modules:
  0.0 665.1 jit_solution(10254820897277295761)
XLA Ops:
  7.2 0.0 all-gather.3.cloned.1.call-start
  7.2 0.7 all-gather.3.cloned.1.call-update
  7.9 0.0 all-gather.5.cloned.1.call-start
  7.9 0.7 and_select_fusion.2
  8.6 0.7 fusion.5
  9.3 0.8 convolution_bitcast_fusion.1
  10.1 33.9 %psum.7 = f32[8]{0:T(128)S(1)} all-reduce(f32[8]{0:T(128)S(1)} %convolution_bitcast_fusion.1), channel_id=1, replica_groups=mesh['ia'=2,'ja'=8,'ka'=8] {'ia','ka'}, use_global_device_ids=true, to_apply=%region_2.3 | all-reduce | flops 8 | bytes 64 | tf_op jit(solution)/shard_map/psum | solution.py:71
  44.0 0.2 fusion.1
  44.2 1.7 multiply_convert_fusion
  45.9 0.0 all-gather.5.cloned.1.call-update
  46.0 0.0 reduce-scatter.5.cloned.1.call-start
  46.0 81.2 %all-gather.3.cloned.1.call-done = bf16[768,3328]{1,0:T(8,128)(2,1)} async-done(((bf16[48,3328]{1,0:T(8,128)(2,1)}), bf16[768,3328]{1,0:T(8,128)(2,1)}) %all-gather.3.cloned.1.call-update) | async-done | bytes 5111824 | tf_op jit(solution)/shard_map/all_gather | solution.py:17
  127.2 10.2 %fusion.19 = f32[768,1024]{1,0:T(8,128)} fusion(bf16[768,3328]{1,0:T(8,128)(2,1)} %all-gather.3.cloned.1.call-done, bf16[3328,1024]{1,0:T(8,128)(2,1)} %param.8), kind=kOutput, calls=%fused_computation.35 | convolution fusion | flops 5234491392 | bytes 15073280 | tf_op jit(solution)/shard_map/dot_general | solution.py:57
  137.4 0.0 reduce-scatter.5.cloned.1.call-update
  137.5 0.0 reduce-scatter.9.cloned.1.call-start
  137.5 68.5 %all-gather.5.cloned.1.call-done = bf16[768,2048]{1,0:T(8,128)(2,1)} async-done(((bf16[48,2048]{1,0:T(8,128)(2,1)}), bf16[768,2048]{1,0:T(8,128)(2,1)}) %all-gather.5.cloned.1.call-update) | async-done | bytes 3145744 | tf_op jit(solution)/shard_map/all_gather | solution.py:17
  206.0 8.3 %fusion.21 = f32[768,1024]{1,0:T(8,128)} fusion(bf16[768,2048]{1,0:T(8,128)(2,1)} %all-gather.5.cloned.1.call-done, bf16[1024,2048]{1,0:T(8,128)(2,1)} %param.9), kind=kOutput, calls=%fused_computation.37 | convolution fusion | flops 3221225472 | bytes 10485760 | tf_op jit(solution)/shard_map/dot_general | solution.py:40
  214.2 0.0 reduce-scatter.9.cloned.1.call-update
  214.3 0.0 reduce-scatter.7.cloned.1.call-start
  214.3 31.8 %reduce-scatter.5.cloned.1.call-done = f32[96,1024]{1,0:T(8,128)} async-done(((f32[768,1024]{1,0:T(8,128)}), f32[96,1024]{1,0:T(8,128)}) %reduce-scatter.5.cloned.1.call-update) | async-done | bytes 393232 | tf_op jit(solution)/shard_map/reduce_scatter | solution.py:30
  246.1 0.0 copy-start
  246.1 1.2 convert_element_type.34
  247.3 0.2 tile.4
  247.4 32.5 %all_to_all.18 = bf16[8,96,1024]{2,1,0:T(8,128)(2,1)S(1)} all-to-all(bf16[8,96,1024]{2,1,0:T(8,128)(2,1)S(1)} %tile.4), channel_id=1, replica_groups=mesh['ia'=2,'ja'=8,'ka'=8] {'ja'}, dimensions={0} | all-to-all | bytes 3145728 | tf_op jit(solution)/shard_map/all_to_all | solution.py:13
  279.9 0.0 copy-done
  279.9 5.4 fusion.20
  285.3 0.0 reduce-scatter.7.cloned.1.call-update
  285.3 0.0 reduce-scatter.11.cloned.1.call-start
  285.4 8.4 %reduce-scatter.9.cloned.1.call-done = f32[96,1024]{1,0:T(8,128)} async-done(((f32[768,1024]{1,0:T(8,128)}), f32[96,1024]{1,0:T(8,128)}) %reduce-scatter.9.cloned.1.call-update) | async-done | bytes 393232 | tf_op jit(solution)/shard_map/reduce_scatter | solution.py:30
  293.8 1.0 convert_element_type.40
  294.8 0.2 tile.5
  295.0 25.9 %all_to_all.19 = bf16[8,96,1024]{2,1,0:T(8,128)(2,1)S(1)} all-to-all(bf16[8,96,1024]{2,1,0:T(8,128)(2,1)S(1)} %tile.5), channel_id=1, replica_groups=mesh['ia'=2,'ja'=8,'ka'=8] {'ja'}, dimensions={0} | all-to-all | bytes 3145728 | tf_op jit(solution)/shard_map/all_to_all | solution.py:13
  320.9 11.0 %fusion.22 = f32[768,3328]{1,0:T(8,128)} fusion(bf16[768,1024]{1,0:T(8,128)(2,1)S(1)} %bitcast.30, bf16[3328,1024]{1,0:T(8,128)(2,1)} %param.8), kind=kOutput, calls=%fused_computation.38 | convolution fusion | flops 5234491392 | bytes 18612224 | tf_op jit(solution)/shard_map/dot_general | solution.py:40
  331.9 0.0 reduce-scatter.11.cloned.1.call-update
  332.0 9.9 %fusion = bf16[3328,1024]{0,1:T(8,128)(2,1)} fusion(bf16[768,1024]{1,0:T(8,128)(2,1)S(1)} %bitcast.31, bf16[768,3328]{1,0:T(8,128)(2,1)} %all-gather.3.cloned.1.call-done), kind=kOutput, calls=%fused_computation.1 | convolution fusion | flops 5237899264 | bytes 13500416 | tf_op jit(solution)/shard_map/dot_general | solution.py:46
  341.9 9.9 %copy.11 = bf16[3328,1024]{1,0:T(8,128)(2,1)} copy(bf16[3328,1024]{0,1:T(8,128)(2,1)} %fusion) | data formatting | bytes 13631488
  351.8 6.9 %convolution_convert_fusion.1 = bf16[1024,2048]{1,0:T(8,128)(2,1)} fusion(bf16[768,1024]{1,0:T(8,128)(2,1)S(1)} %bitcast.29, bf16[768,2048]{1,0:T(8,128)(2,1)} %all-gather.5.cloned.1.call-done), kind=kOutput, calls=%fused_computation.2 | convolution fusion | flops 3223322624 | bytes 8912896 | tf_op jit(solution)/shard_map/dot_general | solution.py:46
  358.8 77.2 %reduce-scatter.7.cloned.1.call-done = f32[48,2048]{1,0:T(8,128)} async-done(((f32[768,2048]{1,0:T(8,128)}), f32[48,2048]{1,0:T(8,128)}) %reduce-scatter.7.cloned.1.call-update) | async-done | bytes 393232 | tf_op jit(solution)/shard_map/reduce_scatter | solution.py:21
  436.0 1.7 convert_element_type.35
  437.7 218.8 %reduce-scatter.11.cloned.1.call-done = f32[48,3328]{1,0:T(8,128)} async-done(((f32[768,3328]{1,0:T(8,128)}), f32[48,3328]{1,0:T(8,128)}) %reduce-scatter.11.cloned.1.call-update) | async-done | bytes 638992 | tf_op jit(solution)/shard_map/reduce_scatter | solution.py:21
  656.5 1.8 convert_element_type.41
Async XLA Ops:
  7.2 120.0 %all-gather.3.cloned.1.call-start = ((), (), s32[]{:S(2)}) async-start(), calls=%async_computation.6 | async-start | bytes 5431296 | tf_op jit(solution)/shard_map/all_gather | solution.py:17
  7.9 198.1 %all-gather.5.cloned.1.call-start = ((), (), s32[]{:S(2)}) async-start(), calls=%async_computation.9 | async-start | bytes 3342336 | tf_op jit(solution)/shard_map/all_gather | solution.py:17
  46.0 200.1 %reduce-scatter.5.cloned.1.call-start = ((), (), s32[]{:S(2)}) async-start(), calls=%async_computation.7 | async-start | bytes 3538944 | tf_op jit(solution)/shard_map/reduce_scatter | solution.py:30
  137.5 156.4 %reduce-scatter.9.cloned.1.call-start = ((), (), s32[]{:S(2)}) async-start(), calls=%async_computation.10 | async-start | bytes 3538944 | tf_op jit(solution)/shard_map/reduce_scatter | solution.py:30
  214.3 221.7 %reduce-scatter.7.cloned.1.call-start = ((), (), s32[]{:S(2)}) async-start(), calls=%async_computation.8 | async-start | bytes 6684672 | tf_op jit(solution)/shard_map/reduce_scatter | solution.py:21
  246.1 33.8 %copy-start = (bf16[1024,2048]{1,0:T(8,128)(2,1)S(1)}, bf16[1024,2048]{1,0:T(8,128)(2,1)}, u32[]{:S(2)}) copy-start(bf16[1024,2048]{1,0:T(8,128)(2,1)} %param.9) | copy-start | bytes 12582916
  285.3 371.1 %reduce-scatter.11.cloned.1.call-start = ((), (), s32[]{:S(2)}) async-start(), calls=%async_computation.11 | async-start | bytes 10862592 | tf_op jit(solution)/shard_map/reduce_scatter | solution.py:21
Sparse Core Ops, SparseCore 0:
  9.6 117.5 all-gather.2
  129.4 76.5 all-gather.4
  209.0 37.0 reduce-scatter.4
  248.9 44.8 reduce-scatter.8
  296.1 139.8 reduce-scatter.6
  438.3 218.1 reduce-scatter.10
